TPU v7x, 32 devices: a whole 2x2x4 slice. The times are simulated.
32 devices in a mesh: grp: 2 (over y), slab: 4 (over z), mem: 2 (over x), sub: 2 (over core).
Axes of the slice: x: 2, y: 2, z: 4, core: 2. Of those that a mesh axis runs over, the one named last changes fastest.
Arguments:
- state: bfloat16 [256, 32768], P('mem', ('grp', 'slab', 'sub')), parts along dimension 1, may hold values from -6 to 6
- centers: int32 [512], P('grp'), parts along dimension 0, may hold values from 0 to 16383, as said below
- half_width: int32 [512], P('grp'), parts along dimension 0, may hold values from 4 to 71
- radius: int32 [512], P('grp'), parts along dimension 0, may hold values from 2048 to 8192
- order: int32 [512], P('grp'), parts along dimension 0, may hold values from 0 to 255, each once
- obs_var: float32 [512], P('grp'), parts along dimension 0, may hold values from 0.1 to 1
Outputs:
- analysis: bfloat16 [256, 32768], P('mem', ('grp', 'slab', 'sub')), parts along dimension 1
There are 2 independent parts, one for each index of `grp`. A program takes and returns all parts, laid end to end along the dimension named above; each array names one. Nothing has to cross between parts.
Inputs may be any that keep to these rules, and one draw needn't show every extreme that they name: order holds every observation number once. Observations 4 k to 4 k + 3 have centers within 6 rows of a common site row, which the first of them sits on; centers are clipped to the grid.
All inputs are finite; a program needn't handle non-finite values.
Results may differ from a plain program's by a relative error of at most 0.0049.
Values may be sent and summed in bfloat16 or wider, within the bound.
A program may use at most 64 MiB of HBM per device.

v0:
```python
import math
import jax
import jax.numpy as jnp
from jax import lax
from jax.sharding import PartitionSpec as P

M = 256
P_SIZE = 128
BATCHES = 2
floor_level = math.exp(-2.0)


def geometry(first_row, row_count, center_rows, half_rows, radius_rows):
    rows_all = first_row + lax.iota(jnp.int32, row_count)
    distance = (rows_all[None, :] - center_rows[:, None]).astype(jnp.float32)
    half_f = half_rows.astype(jnp.float32)[:, None]
    footprint = (
        jnp.maximum(jnp.exp(-2.0 * distance * distance / (half_f * half_f)) - floor_level, 0.0)
        / jnp.sqrt(half_f)
    ).astype(jnp.bfloat16)
    taper_rows = jnp.square(
        jnp.maximum(1.0 - jnp.abs(distance) / radius_rows.astype(jnp.float32)[:, None], 0.0)
    )
    return (footprint, taper_rows)


def gain_terms(projected, variance):
    high = lax.Precision.HIGHEST
    covariance = jnp.dot(
        projected.T, projected, precision=high, preferred_element_type=jnp.float32
    ) / (M - 1) + jnp.diag(variance)
    factor = jnp.linalg.cholesky(covariance)
    identity = jnp.eye(P_SIZE, dtype=jnp.float32)
    inner_inv = lax.linalg.triangular_solve(
        factor + jnp.diag(jnp.sqrt(variance)), identity, left_side=True, lower=True
    )
    gain_mat = lax.linalg.triangular_solve(
        factor, inner_inv, left_side=True, lower=True, transpose_a=True
    )
    weights = jnp.dot(
        projected, gain_mat.T, precision=high, preferred_element_type=jnp.float32
    ).astype(jnp.bfloat16)
    return (weights, projected.astype(jnp.bfloat16))


def project_rows(ensemble, footprint):
    return lax.dot_general(
        ensemble, footprint, (((1,), (1,)), ((), ())), preferred_element_type=jnp.float32
    )


def cross_rows(projected_b, ensemble):
    return lax.dot_general(
        projected_b, ensemble, (((0,), (0,)), ((), ())), preferred_element_type=jnp.float32
    )


def on_device(state, centers, half_width, radius, order, obs_var):
    own_count, rows_here = state.shape
    row_base = lax.axis_index(("slab", "sub")) * rows_here
    centers_all = centers[order]
    half_all = half_width[order]
    radius_all = radius[order]
    variance_all = obs_var[order]
    ensemble = state
    offset = lax.axis_index("mem") * own_count
    for batch in range(BATCHES):
        lo_obs = batch * P_SIZE
        footprint, taper_rows = geometry(
            row_base,
            rows_here,
            centers_all[lo_obs : lo_obs + P_SIZE],
            half_all[lo_obs : lo_obs + P_SIZE],
            radius_all[lo_obs : lo_obs + P_SIZE],
        )
        partial_value = project_rows(ensemble, footprint)
        summed_own = lax.psum(partial_value, ("slab", "sub"))
        projected = lax.all_gather(summed_own, "mem", axis=0, tiled=True)
        weights, projected_b = gain_terms(projected, variance_all[lo_obs : lo_obs + P_SIZE])
        cross_cov = cross_rows(projected_b, lax.all_gather(ensemble, "mem", axis=0, tiled=True))
        tapered = (taper_rows * cross_cov / (M - 1)).astype(jnp.bfloat16)
        weights_own = lax.dynamic_slice_in_dim(weights, offset, own_count, 0)
        ensemble = (
            ensemble.astype(jnp.float32)
            - jnp.dot(weights_own, tapered, preferred_element_type=jnp.float32)
        ).astype(jnp.bfloat16)
    return ensemble


def solution(mesh):
    placed = (P("mem", ("grp", "slab", "sub")), P("grp"), P("grp"), P("grp"), P("grp"), P("grp"))
    return jax.shard_map(
        on_device,
        mesh=mesh,
        in_specs=placed,
        out_specs=P("mem", ("grp", "slab", "sub")),
        check_vma=False,
    )
```

profile of v0, /device:TPU:0, one launch (start us, length us, event | category | flops | bytes accessed | tf_op | source)
XLA Modules:
  0.0 215.7 jit_solution(16010699349236108994)
XLA Ops:
  7.4 0.7 copy-done.8
  8.1 1.9 gather_fusion.1
  10.1 0.7 copy-done.1
  10.7 1.9 gather_fusion
  12.7 1.2 convolution_bitcast_fusion
  15.2 1.9 gather_fusion.2
  17.2 0.7 copy-done.3
  17.9 1.9 gather_fusion.3
  19.8 50.6 %all-reduce.3.cloned.1.call-done = f32[128,128]{0,1:T(8,128)} async-done(((f32[128,128]{0,1:T(8,128)}), f32[128,128]{0,1:T(8,128)}) %all-reduce.3.cloned.1.call-update) | async-done | bytes 65552 | tf_op jit(solution)/shard_map/psum | solution.py:77
  70.4 5.3 %all_gather.12 = f32[256,128]{0,1:T(8,128)S(1)} all-gather(f32[128,128]{0,1:T(8,128)} %all-reduce.3.cloned.1.call-done), channel_id=1, replica_groups=mesh['grp'=2,'slab'=4,'mem'=2,'sub'=2] {'mem'}, dimensions={0}, use_global_device_ids=true | all-gather | bytes 196608 | tf_op jit(solution)/shard_map/all_gather | solution.py:78
  76.2 11.7 %cholesky.44 = f32[128,128]{1,0:T(8,128)S(1)} custom-call(f32[128,128]{1,0:T(8,128)S(1)} %copy.12), custom_call_target="Cholesky" | custom-call | tf_op jit(solution)/shard_map/jit(cholesky)/cholesky | solution.py:32
  88.6 0.7 select_bitcast_fusion.2
  89.4 9.8 %custom-call.10 = f32[1,128,128]{1,2,0:T(8,128)S(1)} custom-call(f32[1,128,128]{2,1,0:T(8,128)S(1)} %get-tuple-element.11), custom_call_target="InvertDiagBlocksLowerTriangular" | custom-call | tf_op jit(solution)/shard_map/triangular_solve/custom-call.0 | solution.py:34
  99.2 9.8 %custom-call.11 = f32[1,128,128]{1,2,0:T(8,128)S(1)} custom-call(f32[1,128,128]{2,1,0:T(8,128)S(1)} %get-tuple-element.10), custom_call_target="InvertDiagBlocksLowerTriangular" | custom-call | tf_op jit(solution)/shard_map/triangular_solve/custom-call.2 | solution.py:37
  109.9 2.0 fusion.4
  111.9 1.3 fusion.35
  113.8 52.2 %all-reduce.5.cloned.1.call-done = f32[128,128]{1,0:T(8,128)} async-done(((f32[128,128]{1,0:T(8,128)}), f32[128,128]{1,0:T(8,128)}) %all-reduce.5.cloned.1.call-update) | async-done | bytes 65552 | tf_op jit(solution)/shard_map/psum | solution.py:77
  166.0 5.4 %all_gather.14 = f32[256,128]{1,0:T(8,128)S(1)} all-gather(f32[128,128]{1,0:T(8,128)} %all-reduce.5.cloned.1.call-done), channel_id=1, replica_groups=mesh['grp'=2,'slab'=4,'mem'=2,'sub'=2] {'mem'}, dimensions={0}, use_global_device_ids=true | all-gather | bytes 196608 | tf_op jit(solution)/shard_map/all_gather | solution.py:78
  171.9 11.7 %cholesky.55 = f32[128,128]{1,0:T(8,128)S(1)} custom-call(f32[128,128]{1,0:T(8,128)S(1)} %copy.14), custom_call_target="Cholesky" | custom-call | tf_op jit(solution)/shard_map/jit(cholesky)/cholesky | solution.py:32
  183.7 0.7 compare_reduce_fusion
  184.4 0.7 select_bitcast_fusion
  185.1 9.8 %custom-call.12 = f32[1,128,128]{1,2,0:T(8,128)S(1)} custom-call(f32[1,128,128]{2,1,0:T(8,128)S(1)} %get-tuple-element.8), custom_call_target="InvertDiagBlocksLowerTriangular" | custom-call | tf_op jit(solution)/shard_map/triangular_solve/custom-call.0 | solution.py:34
  194.9 9.8 %custom-call.13 = f32[1,128,128]{1,2,0:T(8,128)S(1)} custom-call(f32[1,128,128]{2,1,0:T(8,128)S(1)} %get-tuple-element.6), custom_call_target="InvertDiagBlocksLowerTriangular" | custom-call | tf_op jit(solution)/shard_map/triangular_solve/custom-call.2 | solution.py:37
  205.5 2.8 %fusion.5 = bf16[128,2048]{1,0:T(8,128)(2,1)} fusion(bf16[256,2048]{1,0:T(8,128)(2,1)} %all-gather.5.cloned.1.call-done, bf16[128,2048]{1,0:T(8,128)(2,1)S(1)} %copy-done.7, f32[128]{0:T(128)S(1)} %get-tuple-element.22, s32[128]{0:T(128)S(1)} %get-tuple-element.20, s32[2048]{0:T(1024)S(1)} %iota_add_fusion, f32[256,128]{1,0:T(8,128)S(1)} %all_gather.14, ...), kind=kOutput, calls=%fused_computation.13 | convolution fusion | flops 204767232 | bytes 2270212 | tf_op jit(solution)/shard_map/dot_general | solution.py:85
  (49 shorter events, 5.4 us)
Async XLA Ops:
  7.4 0.7 copy-start
  7.4 63.0 %all-reduce.3.cloned.1.call-start = ((), (), s32[]{:S(2)}) async-start(), calls=%async_computation | async-start | bytes 131072 | tf_op jit(solution)/shard_map/psum | solution.py:77
  7.4 0.7 copy-start.8
  10.0 0.7 copy-start.1
  10.7 2.0 copy-start.4
  13.9 96.0 %all-gather.3.cloned.1.call-start = ((), (), s32[]{:S(2)}) async-start(), calls=%async_computation.1 | async-start | bytes 1572864 | tf_op jit(solution)/shard_map/all_gather | solution.py:80
  14.5 0.7 copy-start.2
  14.5 151.4 %all-reduce.5.cloned.1.call-start = ((), (), s32[]{:S(2)}) async-start(), calls=%async_computation.2 | async-start | bytes 131072 | tf_op jit(solution)/shard_map/psum | solution.py:77
  17.2 0.7 copy-start.3
  76.1 33.8 %copy-start.5 = (bf16[128,2048]{1,0:T(8,128)(2,1)S(1)}, bf16[128,2048]{1,0:T(8,128)(2,1)}, u32[]{:S(2)}) copy-start(bf16[128,2048]{1,0:T(8,128)(2,1)} %param.11) | copy-start | bytes 1572868
  111.9 1.3 copy-start.6
  113.2 92.3 %all-gather.5.cloned.1.call-start = ((), (), s32[]{:S(2)}) async-start(), calls=%async_computation.3 | async-start | bytes 1572864 | tf_op jit(solution)/shard_map/all_gather | solution.py:80
  171.8 33.7 %copy-start.7 = (bf16[128,2048]{1,0:T(8,128)(2,1)S(1)}, bf16[128,2048]{1,0:T(8,128)(2,1)}, u32[]{:S(2)}) copy-start(bf16[128,2048]{1,0:T(8,128)(2,1)} %copy-done.6) | copy-start | bytes 1572868
Sparse Core Ops, SparseCore 0:
  14.1 56.3 all-reduce.2
  113.3 52.5 all-reduce.4
Sparse Core Ops, SparseCore 1:
  16.0 23.9 all-gather.2
  115.3 20.2 all-gather.4
where the time goes:
time: 216 us
  waiting for transfers between devices  104 us (48%)
  other arithmetic  65.5 us (30%)
  between operations  15.2 us (7%)
  local copies, waits for them, and re-layouts  10.8 us (5%)
  blocking collectives  10.7 us (5%)
  matrix products  9.54 us (4%)
    psum x2, waiting for transfers between devices, on_device(): summed_own = lax.psum(partial_value, ('slab', 'sub'))  103 us
    another operation x6, other arithmetic, gain_terms(): factor = jnp.linalg.cholesky(covariance)  24.8 us
    another operation x4, other arithmetic, gain_terms(): lax.linalg.triangular_solve(factor, inner_inv, left_side=True, lower=True...  21 us
    another operation x2, other arithmetic, gain_terms(): lax.linalg.triangular_solve(factor + jnp.diag(jnp.sqrt(variance)), identi...  19.6 us
    all_gather x2, blocking collectives, on_device(): projected = lax.all_gather(summed_own, 'mem', axis=0, tiled=True)  10.7 us
    dot_general x2, matrix products, on_device(): jnp.dot(weights_own, tapered, preferred_element_type=jnp.float32)  4.76 us
  transfers between devices with their start and end apart: 4, of which 2 were waited for; matrix products, arithmetic and copies ran while one was open for 33% of the time, Pallas kernels for 0%

commit v1 on v0

--- a/solution.py
+++ b/solution.py
@@ -74,7 +74,8 @@
             radius_all[lo_obs : lo_obs + P_SIZE],
         )
         partial_value = project_rows(ensemble, footprint)
-        summed_own = lax.psum(partial_value, ("slab", "sub"))
+        parts = lax.all_gather(partial_value, ("slab", "sub"))
+        summed_own = jnp.sum(parts, axis=0)
         projected = lax.all_gather(summed_own, "mem", axis=0, tiled=True)
         weights, projected_b = gain_terms(projected, variance_all[lo_obs : lo_obs + P_SIZE])
         cross_cov = cross_rows(projected_b, lax.all_gather(ensemble, "mem", axis=0, tiled=True))

time: 216 us -> 144 us (0.67)
  waiting for transfers between devices: 104 us -> 0.77 us
  blocking collectives: 10.7 us -> 43.6 us
    psum x2 -> x0, waiting for transfers between devices: 103 us -> none  [on_device(): summed_own = lax.psum(partial_value, ('slab', 'sub'))]
    all_gather x0 -> x2, blocking collectives: none -> 31.4 us  [on_device(): parts = lax.all_gather(partial_value, ('slab', 'sub'))]
  transfers between devices with their start and end apart: 4 -> 2, of which waited for: 2 -> 0; matrix products, arithmetic and copies ran while one was open for 33% -> 54% of each run, Pallas kernels for 0% -> 0%
where the time goes in v1:
time: 144 us
  other arithmetic  65.7 us (46%)
  blocking collectives  43.6 us (30%)
  between operations  13.7 us (10%)
  local copies, waits for them, and re-layouts  11.3 us (8%)
  matrix products  9.06 us (6%)
    all_gather x2, blocking collectives, on_device(): parts = lax.all_gather(partial_value, ('slab', 'sub'))  31.4 us
    another operation x6, other arithmetic, gain_terms(): factor = jnp.linalg.cholesky(covariance)  24.8 us
    another operation x4, other arithmetic, gain_terms(): lax.linalg.triangular_solve(factor, inner_inv, left_side=True, lower=True...  21.1 us
    another operation x2, other arithmetic, gain_terms(): lax.linalg.triangular_solve(factor + jnp.diag(jnp.sqrt(variance)), identi...  19.6 us
    all_gather x2, blocking collectives, on_device(): projected = lax.all_gather(summed_own, 'mem', axis=0, tiled=True)  12.1 us
    dot_general x2, matrix products, on_device(): jnp.dot(weights_own, tapered, preferred_element_type=jnp.float32)  5.54 us
    unnamed x15, local copies, waits for them, and re-layouts  3.12 us
  transfers between devices with their start and end apart: 2, of which 0 were waited for; matrix products, arithmetic and copies ran while one was open for 54% of the time, Pallas kernels for 0%

profile of v1, /device:TPU:0, one launch (start us, length us, event | category | flops | bytes accessed | tf_op | source)
XLA Modules:
  0.0 144.1 jit_solution(18310845273632824136)
XLA Ops:
  6.5 0.7 all-gather.5.cloned.1.call-update
  7.3 0.7 copy-done.6
  8.0 1.9 %gather_fusion.1 = s32[256]{0:T(256)S(1)} fusion(s32[256]{0:T(256)S(1)} %copy-done, s32[1024]{0:T(1024)S(1)} %pad_clamp_fusion), kind=kCustom, calls=%fused_computation.1 | custom fusion | bytes 3072 | tf_op jit(solution)/shard_map/gather | solution.py:62
  10.0 0.7 copy-done.1
  10.7 1.9 %gather_fusion = s32[256]{0:T(256)S(1)} fusion(s32[256]{0:T(256)S(1)} %copy-done.1, s32[1024]{0:T(1024)S(1)} %pad_clamp_fusion), kind=kCustom, calls=%fused_computation | custom fusion | bytes 3072 | tf_op jit(solution)/shard_map/gather | solution.py:61
  13.2 16.5 %all-gather = f32[1024,128]{0,1:T(8,128)S(1)} all-gather(f32[128,128]{0,1:T(8,128)S(1)} %convolution_bitcast_fusion), channel_id=2, replica_groups=mesh['grp'=2,'slab'=4,'mem'=2,'sub'=2] {'slab','sub'}, dimensions={0}, use_global_device_ids=true | all-gather | bytes 589824 | tf_op jit(solution)/shard_map/all_gather | solution.py:77
  29.9 5.2 %all_gather.26 = f32[256,128]{0,1:T(8,128)S(1)} all-gather(f32[128,128]{0,1:T(8,128)S(1)} %bitcast_reduce_fusion), channel_id=1, replica_groups=mesh['grp'=2,'slab'=4,'mem'=2,'sub'=2] {'mem'}, dimensions={0}, use_global_device_ids=true | all-gather | bytes 196608 | tf_op jit(solution)/shard_map/all_gather | solution.py:79
  35.1 1.9 %gather_fusion.2 = f32[256]{0:T(256)S(1)} fusion(f32[256]{0:T(256)S(1)} %copy-done.2, s32[1024]{0:T(1024)S(1)} %pad_clamp_fusion), kind=kCustom, calls=%fused_computation.2 | custom fusion | bytes 3072 | tf_op jit(solution)/shard_map/gather | solution.py:64
  37.6 11.7 %cholesky.44 = f32[128,128]{1,0:T(8,128)S(1)} custom-call(f32[128,128]{1,0:T(8,128)S(1)} %copy.16), custom_call_target="Cholesky" | custom-call | tf_op jit(solution)/shard_map/jit(cholesky)/cholesky | solution.py:32
  50.0 0.7 select_bitcast_fusion.2
  50.7 9.8 %custom-call.10 = f32[1,128,128]{1,2,0:T(8,128)S(1)} custom-call(f32[1,128,128]{2,1,0:T(8,128)S(1)} %get-tuple-element.11), custom_call_target="InvertDiagBlocksLowerTriangular" | custom-call | tf_op jit(solution)/shard_map/triangular_solve/custom-call.0 | solution.py:34
  60.5 9.8 %custom-call.11 = f32[1,128,128]{1,2,0:T(8,128)S(1)} custom-call(f32[1,128,128]{2,1,0:T(8,128)S(1)} %get-tuple-element.10), custom_call_target="InvertDiagBlocksLowerTriangular" | custom-call | tf_op jit(solution)/shard_map/triangular_solve/custom-call.2 | solution.py:37
  70.4 0.7 copy-done.3
  71.1 1.9 %gather_fusion.3 = s32[256]{0:T(256)S(1)} fusion(s32[256]{0:T(256)S(1)} %copy-done.3, s32[1024]{0:T(1024)S(1)} %pad_clamp_fusion), kind=kCustom, calls=%fused_computation.3 | custom fusion | bytes 3072 | tf_op jit(solution)/shard_map/gather | solution.py:63
  73.9 2.8 %fusion.4 = bf16[128,2048]{1,0:T(8,128)(2,1)} fusion(bf16[256,2048]{1,0:T(8,128)(2,1)} %all-gather.5.cloned.1.call-done, bf16[128,2048]{1,0:T(8,128)(2,1)S(1)} %copy-done.4, f32[128]{0:T(128)S(1)} %get-tuple-element.23, s32[128]{0:T(128)S(1)} %get-tuple-element.21, s32[2048]{0:T(1024)S(1)} %iota_add_fusion, f32[256,128]{0,1:T(8,128)S(1)} %all_gather.26, ...), kind=kOutput, calls=%fused_computation.12 | convolution fusion | flops 204767232 | bytes 2270212 | tf_op jit(solution)/shard_map/dot_general | solution.py:86
  76.7 1.0 copy-done.5
  78.4 14.9 %all-gather.1 = f32[1024,128]{1,0:T(8,128)S(1)} all-gather(f32[128,128]{1,0:T(8,128)S(1)} %fusion.35), channel_id=3, replica_groups=mesh['grp'=2,'slab'=4,'mem'=2,'sub'=2] {'slab','sub'}, dimensions={0}, use_global_device_ids=true | all-gather | bytes 589824 | tf_op jit(solution)/shard_map/all_gather | solution.py:77
  93.3 6.9 %all_gather.30 = f32[256,128]{1,0:T(8,128)S(1)} all-gather(f32[128,128]{1,0:T(8,128)S(1)} %reduce_sum.19), channel_id=1, replica_groups=mesh['grp'=2,'slab'=4,'mem'=2,'sub'=2] {'mem'}, dimensions={0}, use_global_device_ids=true | all-gather | bytes 196608 | tf_op jit(solution)/shard_map/all_gather | solution.py:79
  100.9 11.7 %cholesky.55 = f32[128,128]{1,0:T(8,128)S(1)} custom-call(f32[128,128]{1,0:T(8,128)S(1)} %copy.18), custom_call_target="Cholesky" | custom-call | tf_op jit(solution)/shard_map/jit(cholesky)/cholesky | solution.py:32
  112.6 0.7 compare_reduce_fusion
  113.3 0.7 select_bitcast_fusion
  114.0 9.8 %custom-call.12 = f32[1,128,128]{1,2,0:T(8,128)S(1)} custom-call(f32[1,128,128]{2,1,0:T(8,128)S(1)} %get-tuple-element.8), custom_call_target="InvertDiagBlocksLowerTriangular" | custom-call | tf_op jit(solution)/shard_map/triangular_solve/custom-call.0 | solution.py:34
  123.8 9.8 %custom-call.13 = f32[1,128,128]{1,2,0:T(8,128)S(1)} custom-call(f32[1,128,128]{2,1,0:T(8,128)S(1)} %get-tuple-element.6), custom_call_target="InvertDiagBlocksLowerTriangular" | custom-call | tf_op jit(solution)/shard_map/triangular_solve/custom-call.2 | solution.py:37
  134.5 2.8 %fusion.5 = bf16[128,2048]{1,0:T(8,128)(2,1)} fusion(bf16[256,2048]{1,0:T(8,128)(2,1)} %all-gather.7.cloned.1.call-done, bf16[128,2048]{1,0:T(8,128)(2,1)S(1)} %copy-done.5, f32[128]{0:T(128)S(1)} %get-tuple-element.22, s32[128]{0:T(128)S(1)} %get-tuple-element.20, s32[2048]{0:T(1024)S(1)} %iota_add_fusion, f32[256,128]{1,0:T(8,128)S(1)} %all_gather.30, ...), kind=kOutput, calls=%fused_computation.13 | convolution fusion | flops 204767232 | bytes 2270212 | tf_op jit(solution)/shard_map/dot_general | solution.py:86
  (44 shorter events, 5.0 us)
Async XLA Ops:
  6.5 1.5 %copy-start = (s32[256]{0:T(256)S(1)}, s32[256]{0:T(256)}, u32[]{:S(2)}) copy-start(s32[256]{0:T(256)} %param.13) | copy-start | bytes 3076
  6.5 67.4 %all-gather.5.cloned.1.call-start = ((), (), s32[]{:S(2)}) async-start(), calls=%async_computation | async-start | bytes 1572864 | tf_op jit(solution)/shard_map/all_gather | solution.py:81
  7.3 127.2 %all-gather.7.cloned.1.call-start = ((), (), s32[]{:S(2)}) async-start(), calls=%async_computation.1 | async-start | bytes 1572864 | tf_op jit(solution)/shard_map/all_gather | solution.py:81
  7.3 0.7 copy-start.6
  10.0 0.7 copy-start.1
  10.6 2.0 %copy-start.4 = (bf16[128,2048]{1,0:T(8,128)(2,1)S(1)}, bf16[128,2048]{1,0:T(8,128)(2,1)}, u32[]{:S(2)}) copy-start(bf16[128,2048]{1,0:T(8,128)(2,1)} %param.11) | copy-start | bytes 1572868
  29.9 5.2 %copy-start.2 = (f32[256]{0:T(256)S(1)}, f32[256]{0:T(256)}, u32[]{:S(2)}) copy-start(f32[256]{0:T(256)} %param.16) | copy-start | bytes 3076
  70.4 0.7 copy-start.3
  76.7 1.0 copy-start.5
Sparse Core Ops, SparseCore 0:
  8.9 23.9 all-gather.4
  76.8 23.8 all-gather.6
